TPU v7x, 256 devices: a whole 4x4x8 slice. The times are simulated.
256 devices in a mesh: dp: 32 (over x_hi, z, core), grp: 8 (over y, x_lo).
Axes of the slice: x: 4 (x_hi: 2, x_lo: 2; x = x_hi * 2 + x_lo), y: 4, z: 8, core: 2. Of those that a mesh axis runs over, the one named last changes fastest.
Arguments:
- images: bfloat16 [16384, 1152], P(('dp', 'grp')), may hold values from -24 to 24
- texts: bfloat16 [16384, 1152], P(('dp', 'grp')), may hold values from -24 to 24
- log_scale: float32 [1], replicated, may hold values from 4 to 4.8
- bias: float32 [1], replicated, may hold values from -12 to -8
Outputs:
- image_grad: float32 [16384, 1152], P(('dp', 'grp'))
- text_grad: float32 [16384, 1152], P(('dp', 'grp'))
- stats: float32 [3], replicated
All inputs are finite; a program needn't handle non-finite values.
Results may differ from a plain program's by a relative error of at most 0.002.
The roundings to bfloat16 on the way count: a program that leaves them out, or rounds other values in their place, can miss the bound.
Values may be sent and summed in bfloat16 or wider, within the bound.
No kernel may reach another device: no remote copies, remote signals or barrier semaphores. Data moves between devices by JAX's collectives and lax.ppermute only.
A program may use at most 64 MiB of HBM per device.

v0:
```python
import jax
import jax.numpy as jnp
from jax import lax
from jax.sharding import PartitionSpec as P

EPS = 1e-06


def normalize(rows):
    values = rows.astype(jnp.float32)
    norms = jnp.sqrt(jnp.sum(values * values, axis=-1, keepdims=True) + EPS)
    return (values / norms, norms)


def project(direction, unit, norms):
    along = jnp.sum(direction * unit, axis=-1, keepdims=True)
    return (direction - unit * along) / norms


def on_device(images, texts, log_scale, bias):
    rows = images.shape[0]
    img_unit, img_norm = normalize(images)
    txt_unit, txt_norm = normalize(texts)
    img_low = img_unit.astype(jnp.bfloat16)
    txt_low = txt_unit.astype(jnp.bfloat16)
    scale = jnp.exp(log_scale[0])
    shift = bias[0]
    dp_index = lax.axis_index("dp")
    grp_index = lax.axis_index("grp")
    block_imgs = lax.all_gather(img_low, "grp", axis=0, tiled=True)
    img_count = block_imgs.shape[0]
    img_pos = lax.broadcasted_iota(jnp.int32, (img_count, 1), 0)
    piece = lax.all_gather(txt_low, "dp", axis=0, tiled=True)
    count = piece.shape[0]
    cosine = jnp.einsum("ie,je->ij", block_imgs, piece, preferred_element_type=jnp.float32)
    scaled = scale * cosine
    logits = scaled + shift
    local = lax.broadcasted_iota(jnp.int32, (1, count), 1) - dp_index * rows
    positive = (local >= 0) & (local < rows) & (img_pos == grp_index * rows + local)
    sign = jnp.where(positive, 1.0, -1.0).astype(jnp.float32)
    losses = jax.nn.softplus(-sign * logits)
    grad = jax.nn.sigmoid(logits) - positive.astype(jnp.float32)
    sums = jnp.stack([jnp.sum(losses), jnp.sum(grad * scaled), jnp.sum(grad)])
    grad_low, sums = (grad.astype(jnp.bfloat16), sums)
    img_acc = jnp.dot(grad_low, piece, preferred_element_type=jnp.float32)
    term = jnp.einsum("ij,ie->je", grad_low, block_imgs, preferred_element_type=jnp.float32)
    txt_acc = term
    img_acc, txt_acc, totals = (img_acc, txt_acc, sums)
    txt_part = lax.psum_scatter(txt_acc, "dp", scatter_dimension=0, tiled=True)
    img_part = lax.psum_scatter(img_acc, "grp", scatter_dimension=0, tiled=True)
    overall = lax.psum(totals, ("dp", "grp"))
    batch_rows = rows * lax.axis_size("dp") * lax.axis_size("grp")
    image_grad = project(scale * img_part, img_unit, img_norm)
    text_grad = project(scale * txt_part, txt_unit, txt_norm)
    return (image_grad, text_grad, overall / batch_rows)


def solution(mesh):
    in_specs = (P(("dp", "grp"), None), P(("dp", "grp"), None), P(), P())
    out_specs = (P(("dp", "grp"), None), P(("dp", "grp"), None), P())
    return jax.shard_map(
        on_device, mesh=mesh, in_specs=in_specs, out_specs=out_specs, check_vma=False
    )
```

profile of v0, /device:TPU:8, one launch (start us, length us, event | category | flops | bytes accessed | tf_op | source)
XLA Modules:
  0.0 395.3 jit_solution(9898853837945935118)
XLA Ops:
  7.2 0.0 all-gather.3.cloned.1.call-start
  7.2 1.0 fusion.6
  8.3 1.7 fusion.12
  9.9 0.0 all-gather.3.cloned.1.call-update
  10.0 0.0 all-gather.5.cloned.1.call-start
  10.0 1.0 fusion.7
  11.1 1.7 fusion.13
  12.8 0.0 all-gather.5.cloned.1.call-update
  12.8 0.0 reduce-scatter.3.cloned.1.call-start
  14.2 41.0 %all-gather.3.cloned.1.call-done = bf16[512,1152]{1,0:T(8,128)(2,1)} async-done(((bf16[64,1152]{1,0:T(8,128)(2,1)}), bf16[512,1152]{1,0:T(8,128)(2,1)}) %all-gather.3.cloned.1.call-update) | async-done | bytes 1179664 | tf_op jit(solution)/shard_map/all_gather | solution.py:30
  55.2 93.0 %all-gather.5.cloned.1.call-done = bf16[2048,1152]{1,0:T(8,128)(2,1)} async-done(((bf16[64,1152]{1,0:T(8,128)(2,1)}), bf16[2048,1152]{1,0:T(8,128)(2,1)}) %all-gather.5.cloned.1.call-update) | async-done | bytes 4718608 | tf_op jit(solution)/shard_map/all_gather | solution.py:33
  148.1 0.0 copy-start.2
  148.1 10.1 %fusion = (f32[]{:T(128)}, f32[]{:T(128)}, f32[]{:T(128)}, f32[512,2048]{1,0:T(8,128)S(1)}) fusion(s32[2048]{0:T(1024)S(1)} %fusion.8, f32[]{:T(128)} %bitcast.10, f32[]{:T(128)} %bitcast, pred[2048]{0:T(1024)(128)(4,1)S(1)} %fusion.11, bf16[512,1152]{1,0:T(8,128)(2,1)} %all-gather.3.cloned.1.call-done, bf16[2048,1152]{1,0:T(8,128)(2,1)} %all-gather.5.cloned.1.call-done), kind=kOutput, calls=%fused_computation.1 | convolution fusion | flops 2438987776 | bytes 10102804 | tf_op jit(solution)/shard_map/ie,je->ij/dot_general | solution.py:35
  158.3 0.0 copy-start.4
  158.3 2.1 copy-done.4
  160.3 0.0 copy-done.2
  160.3 0.0 copy-start.3
  160.3 5.4 %fusion.4 = f32[512,1152]{1,0:T(8,128)} fusion(bf16[2048,1152]{1,0:T(8,128)(2,1)S(1)} %copy-done.2, f32[512,2048]{1,0:T(8,128)S(1)} %get-tuple-element.6, s32[2048]{0:T(1024)S(1)} %fusion.8, f32[]{:T(128)} %bitcast.9, f32[]{:T(128)} %bitcast, pred[2048]{0:T(1024)(128)(4,1)S(1)} %fusion.11), kind=kOutput, calls=%fused_computation.8 | convolution fusion | flops 2426404864 | bytes 11282440 | tf_op jit(solution)/shard_map/dot_general | solution.py:45
  165.8 0.0 reduce-scatter.3.cloned.1.call-update
  165.8 0.0 reduce-scatter.5.cloned.1.call-start
  165.8 0.0 copy-done.3
  165.8 9.8 %fusion.2 = f32[2048,1152]{1,0:T(8,128)} fusion(bf16[512,1152]{1,0:T(8,128)(2,1)S(1)} %copy-done.3, f32[512,2048]{1,0:T(8,128)} %copy-done.4, s32[2048]{0:T(1024)S(1)} %fusion.8, f32[]{:T(128)} %bitcast.11, f32[]{:T(128)} %bitcast, pred[2048]{0:T(1024)(128)(4,1)S(1)} %fusion.11), kind=kOutput, calls=%fused_computation.6 | convolution fusion | flops 2426404864 | bytes 14821384 | tf_op jit(solution)/shard_map/ij,ie->je/dot_general | solution.py:46
  175.6 0.0 copy-start
  175.6 0.0 copy-start.1
  175.6 0.0 reduce-scatter.5.cloned.1.call-update
  175.7 2.0 pad_maximum_fusion
  177.6 75.7 %psum.7 = f32[3]{0:T(128)S(1)} all-reduce(f32[3]{0:T(128)S(1)} %pad_maximum_fusion), channel_id=1, replica_groups=mesh['dp'=32,'grp'=8] {'dp','grp'}, use_global_device_ids=true, to_apply=%region_9.10 | all-reduce | flops 3 | bytes 24 | tf_op jit(solution)/shard_map/psum | solution.py:51
  253.4 0.5 broadcast_multiply_fusion
  253.9 0.0 reduce-scatter.3.cloned.1.call-done
  253.9 0.0 copy-done
  253.9 1.2 multiply_reduce_fusion.2
  255.1 1.8 subtract_divide_fusion.1
  256.9 128.8 %reduce-scatter.5.cloned.1.call-done = f32[64,1152]{1,0:T(8,128)} async-done(((f32[2048,1152]{1,0:T(8,128)}), f32[64,1152]{1,0:T(8,128)}) %reduce-scatter.5.cloned.1.call-update) | async-done | bytes 294928 | tf_op jit(solution)/shard_map/reduce_scatter | solution.py:49
  385.8 0.0 copy-done.1
  385.8 1.2 multiply_reduce_fusion.1
  387.0 1.8 subtract_divide_fusion
  (4 shorter events, 0.0 us)
Async XLA Ops:
  7.2 48.0 %all-gather.3.cloned.1.call-start = ((), (), s32[]{:S(2)}) async-start(), calls=%async_computation.2 | async-start | bytes 1327104 | tf_op jit(solution)/shard_map/all_gather | solution.py:30
  10.0 138.2 %all-gather.5.cloned.1.call-start = ((), (), s32[]{:S(2)}) async-start(), calls=%async_computation.3 | async-start | bytes 4866048 | tf_op jit(solution)/shard_map/all_gather | solution.py:33
  12.8 241.1 %reduce-scatter.3.cloned.1.call-start = ((), (), s32[]{:S(2)}) async-start(), calls=%async_computation.4 | async-start | bytes 2654208 | tf_op jit(solution)/shard_map/reduce_scatter | solution.py:50
  148.1 12.2 %copy-start.2 = (bf16[2048,1152]{1,0:T(8,128)(2,1)S(1)}, bf16[2048,1152]{1,0:T(8,128)(2,1)}, u32[]{:S(2)}) copy-start(bf16[2048,1152]{1,0:T(8,128)(2,1)} %all-gather.5.cloned.1.call-done) | copy-start | bytes 14155780
  158.3 2.1 copy-start.4
  160.3 5.5 %copy-start.3 = (bf16[512,1152]{1,0:T(8,128)(2,1)S(1)}, bf16[512,1152]{1,0:T(8,128)(2,1)}, u32[]{:S(2)}) copy-start(bf16[512,1152]{1,0:T(8,128)(2,1)} %all-gather.3.cloned.1.call-done) | copy-start | bytes 3538948
  165.8 220.0 %reduce-scatter.5.cloned.1.call-start = ((), (), s32[]{:S(2)}) async-start(), calls=%async_computation.5 | async-start | bytes 9732096 | tf_op jit(solution)/shard_map/reduce_scatter | solution.py:49
  175.6 78.3 %copy-start = (bf16[64,1152]{1,0:T(8,128)(2,1)S(1)}, bf16[64,1152]{1,0:T(8,128)(2,1)}, u32[]{:S(2)}) copy-start(bf16[64,1152]{1,0:T(8,128)(2,1)} %param.4) | copy-start | bytes 442372
  175.6 210.2 %copy-start.1 = (bf16[64,1152]{1,0:T(8,128)(2,1)S(1)}, bf16[64,1152]{1,0:T(8,128)(2,1)}, u32[]{:S(2)}) copy-start(bf16[64,1152]{1,0:T(8,128)(2,1)} %param.5) | copy-start | bytes 442372
Sparse Core Ops, SparseCore 0:
  10.4 44.7 all-gather.2
  58.5 89.5 all-gather.4
  165.9 55.6 reduce-scatter.2
  225.9 159.8 reduce-scatter.4
where the time goes:
time: 396 us; the launch traced here: 395 us
  waiting for transfers between devices  263 us (66%)
  blocking collectives  75.7 us (19%)
  matrix products  25.3 us (6%)
  between operations  15.2 us (4%)
  other arithmetic  14 us (4%)
    reduce_scatter x1, waiting for transfers between devices, on_device(): txt_part = lax.psum_scatter(txt_acc, 'dp', scatter_dimension=0, tiled=True)  129 us
    all_gather x1, waiting for transfers between devices, on_device(): piece = lax.all_gather(txt_low, 'dp', axis=0, tiled=True)  93 us
    psum x1, blocking collectives, on_device(): overall = lax.psum(totals, ('dp', 'grp'))  75.7 us
    all_gather x1, waiting for transfers between devices, on_device(): block_imgs = lax.all_gather(img_low, 'grp', axis=0, tiled=True)  41 us
    dot_general x1, matrix products, on_device(): jnp.einsum('ie,je->ij', block_imgs, piece, preferred_element_type=jnp.flo...  10.1 us
    dot_general x1, matrix products, on_device(): jnp.einsum('ij,ie->je', grad_low, block_imgs, preferred_element_type=jnp....  9.78 us
  transfers between devices with their start and end apart: 4, of which 3 were waited for; matrix products, arithmetic and copies ran while one was open for 5% of the time, Pallas kernels for 0%

commit v1 on v0

--- a/solution.py
+++ b/solution.py
@@ -30,7 +30,9 @@
     block_imgs = lax.all_gather(img_low, "grp", axis=0, tiled=True)
     img_count = block_imgs.shape[0]
     img_pos = lax.broadcasted_iota(jnp.int32, (img_count, 1), 0)
-    piece = lax.all_gather(txt_low, "dp", axis=0, tiled=True)
+    piece = jnp.concatenate(
+        lax.all_to_all(jnp.stack([txt_low] * lax.axis_size("dp")), "dp", 0, 0), axis=0
+    )
     count = piece.shape[0]
     cosine = jnp.einsum("ie,je->ij", block_imgs, piece, preferred_element_type=jnp.float32)
     scaled = scale * cosine

time: 396 us -> 383 us (0.967)
  waiting for transfers between devices: 263 us -> 236 us
  starting transfers between devices: 0.16 us -> 11.7 us
    all_gather x1 -> x0, waiting for transfers between devices: 93 us -> none  [on_device(): piece = lax.all_gather(txt_low, 'dp', axis=0, tiled=True)]
    all_to_all x0 -> x1, waiting for transfers between devices: none -> 49.2 us  [on_device(): lax.all_to_all(jnp.stack([txt_low] * lax.axis_size('dp')), 'dp', 0, 0)]
    all_gather x1, waiting for transfers between devices: 41 us -> 56.5 us  [on_device(): block_imgs = lax.all_gather(img_low, 'grp', axis=0, tiled=True)]
    all_to_all x0 -> x1, starting transfers between devices: none -> 11.6 us  [on_device(): lax.all_to_all(jnp.stack([txt_low] * lax.axis_size('dp')), 'dp', 0, 0)]
  transfers between devices with their start and end apart: 4 -> 4, of which waited for: 3 -> 3; matrix products, arithmetic and copies ran while one was open for 5% -> 4% of each run, Pallas kernels for 0% -> 0%
where the time goes in v1:
time: 383 us
  waiting for transfers between devices  236 us (62%)
  blocking collectives  75.6 us (20%)
  matrix products  27.6 us (7%)
  between operations  15.2 us (4%)
  starting transfers between devices  11.7 us (3%)
  other arithmetic  11.5 us (3%)
  local copies, waits for them, and re-layouts  4.9 us (1%)
    reduce_scatter x1, waiting for transfers between devices, on_device(): txt_part = lax.psum_scatter(txt_acc, 'dp', scatter_dimension=0, tiled=True)  130 us
    psum x1, blocking collectives, on_device(): overall = lax.psum(totals, ('dp', 'grp'))  75.6 us
    all_gather x1, waiting for transfers between devices, on_device(): block_imgs = lax.all_gather(img_low, 'grp', axis=0, tiled=True)  56.5 us
    all_to_all x1, waiting for transfers between devices, on_device(): lax.all_to_all(jnp.stack([txt_low] * lax.axis_size('dp')), 'dp', 0, 0)  49.2 us
    all_to_all x1, starting transfers between devices, on_device(): lax.all_to_all(jnp.stack([txt_low] * lax.axis_size('dp')), 'dp', 0, 0)  11.6 us
    dot_general x1, matrix products, on_device(): jnp.einsum('ie,je->ij', block_imgs, piece, preferred_element_type=jnp.flo...  10 us
    dot_general x1, matrix products, on_device(): jnp.einsum('ij,ie->je', grad_low, block_imgs, preferred_element_type=jnp....  9.78 us
    dot_general x1, matrix products, on_device(): img_acc = jnp.dot(grad_low, piece, preferred_element_type=jnp.float32)  7.85 us
  transfers between devices with their start and end apart: 4, of which 3 were waited for; matrix products, arithmetic and copies ran while one was open for 4% of the time, Pallas kernels for 0%

profile of v1, /device:TPU:8, one launch (start us, length us, event | category | flops | bytes accessed | tf_op | source)
XLA Modules:
  0.0 382.7 jit_solution(3272737590777594774)
XLA Ops:
  7.2 1.0 fusion.7
  8.2 1.0 fusion.13
  9.2 2.8 stack.10
  12.1 0.0 copy-start
  12.1 11.6 %all-to-all-start = ((bf16[32,64,1152]{2,1,0:T(8,128)(2,1)}), bf16[32,64,1152]{2,1,0:T(8,128)(2,1)}, u32[]{:S(2)}, u32[]{:S(2)}) async-start(bf16[32,64,1152]{2,1,0:T(8,128)(2,1)} %stack.10), calls=%async_computation | async-start | bytes 9437184 | tf_op jit(solution)/shard_map/all_to_all | solution.py:34
  23.6 0.0 all-gather.2.cloned.1.call-start
  23.7 0.0 copy-done
  23.7 0.1 fusion.6
  23.8 0.8 fusion.12
  24.6 0.0 all-gather.2.cloned.1.call-update
  24.6 0.0 reduce-scatter.3.cloned.1.call-start
  26.0 56.5 %all-gather.2.cloned.1.call-done = bf16[512,1152]{1,0:T(8,128)(2,1)} async-done(((bf16[64,1152]{1,0:T(8,128)(2,1)}), bf16[512,1152]{1,0:T(8,128)(2,1)}) %all-gather.2.cloned.1.call-update) | async-done | bytes 1179664 | tf_op jit(solution)/shard_map/all_gather | solution.py:30
  82.6 49.2 %all-to-all-done = bf16[32,64,1152]{2,1,0:T(8,128)(2,1)} async-done(((bf16[32,64,1152]{2,1,0:T(8,128)(2,1)}), bf16[32,64,1152]{2,1,0:T(8,128)(2,1)}, u32[]{:S(2)}, u32[]{:S(2)}) %all-to-all-start) | async-done | bytes 4718624 | tf_op jit(solution)/shard_map/all_to_all | solution.py:34
  131.8 10.0 %fusion = (f32[]{:T(128)}, f32[]{:T(128)}, f32[]{:T(128)}, f32[512,2048]{1,0:T(8,128)S(1)}) fusion(s32[2048]{0:T(1024)S(1)} %fusion.8, f32[]{:T(128)} %bitcast.11, f32[]{:T(128)} %bitcast, pred[2048]{0:T(1024)(128)(4,1)S(1)} %fusion.11, bf16[512,1152]{1,0:T(8,128)(2,1)} %all-gather.2.cloned.1.call-done, bf16[2048,1152]{1,0:T(8,128)(2,1)} %bitcast.1), kind=kOutput, calls=%fused_computation.1 | convolution fusion | flops 2438987776 | bytes 10102804 | tf_op jit(solution)/shard_map/ie,je->ij/dot_general | solution.py:37
  141.8 0.0 copy-start.3
  141.8 2.1 copy-done.3
  143.9 0.0 copy-start.2
  143.9 7.9 %fusion.4 = f32[512,1152]{1,0:T(8,128)} fusion(bf16[2048,1152]{1,0:T(8,128)(2,1)} %bitcast.1, f32[512,2048]{1,0:T(8,128)S(1)} %get-tuple-element.6, s32[2048]{0:T(1024)S(1)} %fusion.8, f32[]{:T(128)} %bitcast.10, f32[]{:T(128)} %bitcast, pred[2048]{0:T(1024)(128)(4,1)S(1)} %fusion.11), kind=kOutput, calls=%fused_computation.8 | convolution fusion | flops 2426404864 | bytes 11282440 | tf_op jit(solution)/shard_map/dot_general | solution.py:47
  151.7 0.0 reduce-scatter.3.cloned.1.call-update
  151.7 0.0 reduce-scatter.5.cloned.1.call-start
  151.8 0.0 copy-done.2
  151.8 9.8 %fusion.2 = f32[2048,1152]{1,0:T(8,128)} fusion(bf16[512,1152]{1,0:T(8,128)(2,1)S(1)} %copy-done.2, f32[512,2048]{1,0:T(8,128)} %copy-done.3, s32[2048]{0:T(1024)S(1)} %fusion.8, f32[]{:T(128)} %bitcast.12, f32[]{:T(128)} %bitcast, pred[2048]{0:T(1024)(128)(4,1)S(1)} %fusion.11), kind=kOutput, calls=%fused_computation.6 | convolution fusion | flops 2426404864 | bytes 14821384 | tf_op jit(solution)/shard_map/ij,ie->je/dot_general | solution.py:48
  161.6 0.0 copy-start.1
  161.6 0.0 reduce-scatter.5.cloned.1.call-update
  161.6 2.0 pad_maximum_fusion
  163.6 75.6 %psum.7 = f32[3]{0:T(128)S(1)} all-reduce(f32[3]{0:T(128)S(1)} %pad_maximum_fusion), channel_id=1, replica_groups=mesh['dp'=32,'grp'=8] {'dp','grp'}, use_global_device_ids=true, to_apply=%region_9.10 | all-reduce | flops 3 | bytes 24 | tf_op jit(solution)/shard_map/psum | solution.py:53
  239.2 0.5 broadcast_multiply_fusion
  239.7 0.0 reduce-scatter.3.cloned.1.call-done
  239.7 1.2 multiply_reduce_fusion.2
  240.9 1.8 subtract_divide_fusion.1
  242.7 130.4 %reduce-scatter.5.cloned.1.call-done = f32[64,1152]{1,0:T(8,128)} async-done(((f32[2048,1152]{1,0:T(8,128)}), f32[64,1152]{1,0:T(8,128)}) %reduce-scatter.5.cloned.1.call-update) | async-done | bytes 294928 | tf_op jit(solution)/shard_map/reduce_scatter | solution.py:51
  373.2 0.0 copy-done.1
  373.2 1.2 multiply_reduce_fusion.1
  374.3 1.8 subtract_divide_fusion
  (4 shorter events, 0.0 us)
Async XLA Ops:
  12.1 11.6 %copy-start = (bf16[64,1152]{1,0:T(8,128)(2,1)S(1)}, bf16[64,1152]{1,0:T(8,128)(2,1)}, u32[]{:S(2)}) copy-start(bf16[64,1152]{1,0:T(8,128)(2,1)} %param.4) | copy-start | bytes 442372
  12.1 119.7 %all-to-all-start = ((bf16[32,64,1152]{2,1,0:T(8,128)(2,1)}), bf16[32,64,1152]{2,1,0:T(8,128)(2,1)}, u32[]{:S(2)}, u32[]{:S(2)}) async-start(bf16[32,64,1152]{2,1,0:T(8,128)(2,1)} %stack.10), calls=%async_computation | async-start | bytes 9437184 | tf_op jit(solution)/shard_map/all_to_all | solution.py:34
  23.6 58.9 %all-gather.2.cloned.1.call-start = ((), (), s32[]{:S(2)}) async-start(), calls=%async_computation.3 | async-start | bytes 1327104 | tf_op jit(solution)/shard_map/all_gather | solution.py:30
  24.6 215.1 %reduce-scatter.3.cloned.1.call-start = ((), (), s32[]{:S(2)}) async-start(), calls=%async_computation.4 | async-start | bytes 2654208 | tf_op jit(solution)/shard_map/reduce_scatter | solution.py:52
  141.8 2.1 copy-start.3
  143.9 7.9 %copy-start.2 = (bf16[512,1152]{1,0:T(8,128)(2,1)S(1)}, bf16[512,1152]{1,0:T(8,128)(2,1)}, u32[]{:S(2)}) copy-start(bf16[512,1152]{1,0:T(8,128)(2,1)} %all-gather.2.cloned.1.call-done) | copy-start | bytes 3538948
  151.7 221.4 %reduce-scatter.5.cloned.1.call-start = ((), (), s32[]{:S(2)}) async-start(), calls=%async_computation.5 | async-start | bytes 9732096 | tf_op jit(solution)/shard_map/reduce_scatter | solution.py:51
  161.6 211.6 %copy-start.1 = (bf16[64,1152]{1,0:T(8,128)(2,1)S(1)}, bf16[64,1152]{1,0:T(8,128)(2,1)}, u32[]{:S(2)}) copy-start(bf16[64,1152]{1,0:T(8,128)(2,1)} %param.5) | copy-start | bytes 442372
Sparse Core Ops, SparseCore 0:
  26.8 55.6 all-gather.1
  151.9 57.1 reduce-scatter.2
  213.5 159.6 reduce-scatter.4
